TPU v7x, 512 devices: a whole 4x8x8 slice. The times are simulated.
512 devices in a mesh: prow: 16 (over y, core), pcol: 32 (over x, z).
Axes of the slice: x: 4, y: 8, z: 8, core: 2. Of those that a mesh axis runs over, the one named last changes fastest.
Arguments:
- matrix: float32 [2, 4096, 3, 8192], P(None, 'prow', None, 'pcol'), may hold values from -6 to 6
- lower_panel: float32 [2, 4096, 8192], P(None, 'prow', 'pcol'), may hold values from -0.375 to 0.375
- inverses: float32 [2, 256, 256], replicated, as said below
- pivots: int32 [2, 256], replicated, may hold values from 0 to 8191, as said below
- panel_owner: int32 [2], replicated, may hold values from 0 to 31, as said below
Outputs:
- updated: float32 [2, 4096, 3, 8192], P(None, 'prow', None, 'pcol')
Inputs may be any that keep to these rules, and one draw needn't show every extreme that they name: For step s, pivots[s, i] is either s * 256 + i or a row at or after (s + 1) * 256; the entries of one step all differ. panel_owner[1] is panel_owner[0] + 1 modulo 32, and one of the two is 32 - 1. Each inverses[s] is unit lower triangular.
All inputs are finite; a program needn't handle non-finite values.
Results may differ from a plain program's by a relative error of at most 0.0001.
Values sent between devices are 32-bit elements; how exact they have to be, the bound alone decides.
A program may use at most 64 MiB of HBM per device.

v0:
```python
import jax
import jax.numpy as jnp
from jax import lax
from jax.sharding import PartitionSpec as P


def spread(block, axis, holder):
    block = jnp.where(lax.axis_index(axis) == holder, block, jnp.zeros_like(block))
    return lax.psum(block, axis)


def body(matrix, lower_panel, inverses, pivots, panel_owner):
    block_rows, width, block_cols, _ = matrix.shape
    row_count = block_rows * width
    col_count = block_cols * width
    grid_rows = lax.axis_size("prow")
    grid_here = lax.axis_index("prow")
    current = matrix.reshape(row_count, col_count)
    panel_local = lower_panel.reshape(row_count, width)
    local_ids = jnp.arange(row_count, dtype=jnp.int32)
    global_ids = (local_ids // width * grid_rows + grid_here) * width + local_ids % width
    for section in range(2):
        start = section * width
        panel = spread(panel_local, "pcol", panel_owner[section])
        targets = pivots[section]
        target_block = targets // width
        owned = target_block % grid_rows == grid_here
        target_local = target_block // grid_rows * width + targets % width
        safe_rows = jnp.where(owned, target_local, 0)
        offered = jnp.where(owned[:, None], current[safe_rows], 0.0)
        on_diagonal = grid_here == section
        top_block = spread(current[:width], "prow", section)
        picked = lax.psum(offered, "prow")
        upper = jnp.dot(inverses[section], picked, precision=lax.Precision.HIGHEST)
        landing = jnp.where(owned, target_local, row_count)
        current = current.at[landing].set(top_block, mode="drop")
        below = (global_ids >= start + width)[:, None]
        masked = jnp.where(below, panel, 0.0)
        current = current - jnp.dot(masked, upper, precision=lax.Precision.HIGHEST)
        current = current.at[:width].set(jnp.where(on_diagonal, upper, current[:width]))
    return current.reshape(block_rows, width, block_cols, width)


def solution(mesh):
    in_specs = (P(None, "prow", None, "pcol"), P(None, "prow", "pcol"), P(), P(), P())
    out_specs = P(None, "prow", None, "pcol")
    return jax.shard_map(body, mesh=mesh, in_specs=in_specs, out_specs=out_specs, check_vma=False)
```

profile of v0, /device:TPU:1, one launch (start us, length us, event | category | flops | bytes accessed | tf_op | source)
XLA Modules:
  0.0 451.0 jit_solution(13661900788692876497)
XLA Ops:
  6.5 3.8 copy.43
  11.1 2.0 copy.46
  13.4 2.0 gather_fusion
  15.4 1.4 copy.31
  16.8 1.0 broadcast_select_fusion.3
  17.8 0.9 broadcast_select_fusion.2
  20.9 1.1 broadcast_select_fusion.4
  22.1 120.7 %all-reduce.11.cloned.1.call-done = (f32[256,768]{0,1:T(8,128)}, f32[256,768]{0,1:T(8,128)}) async-done(((f32[256,768]{0,1:T(8,128)}, f32[256,768]{0,1:T(8,128)}), (f32[256,768]{0,1:T(8,128)}, f32[256,768]{0,1:T(8,128)})) %all-reduce.11.cloned.1.call-update) | async-done | bytes 1572880 | tf_op jit(solution)/shard_map/psum | solution.py:9
  142.8 1.4 copy.29
  144.2 2.1 scatter_fusion
  146.4 1.6 copy.32
  148.0 0.8 fusion.6
  148.8 155.5 %all-reduce.7.cloned.1.call-done = (f32[512,256]{1,0:T(8,128)}, f32[512,256]{1,0:T(8,128)}) async-done(((f32[512,256]{1,0:T(8,128)}, f32[512,256]{1,0:T(8,128)}), (f32[512,256]{1,0:T(8,128)}, f32[512,256]{1,0:T(8,128)})) %all-reduce.7.cloned.1.call-update) | async-done | bytes 1048592 | tf_op jit(solution)/shard_map/psum | solution.py:9
  304.3 3.1 convolution_subtract_fusion.1
  307.5 1.2 broadcast_select_fusion.1
  309.1 1.1 gather_fusion.1
  310.5 0.9 broadcast_select_fusion
  311.5 120.3 %all-reduce.9.cloned.1.call-done = (f32[256,768]{0,1:T(8,128)}, f32[256,768]{0,1:T(8,128)}) async-done(((f32[256,768]{0,1:T(8,128)}, f32[256,768]{0,1:T(8,128)}), (f32[256,768]{0,1:T(8,128)}, f32[256,768]{0,1:T(8,128)})) %all-reduce.9.cloned.1.call-update) | async-done | bytes 1572880 | tf_op jit(solution)/shard_map/psum | solution.py:9
  431.8 1.4 copy.35
  433.2 2.3 scatter_fusion.1
  435.6 1.6 copy.38
  438.6 2.6 convolution_subtract_fusion
  441.4 1.0 reshape.529
  442.4 2.1 copy.40
  (41 shorter events, 4.2 us)
Async XLA Ops:
  6.5 136.3 %all-reduce.11.cloned.1.call-start = ((), (), s32[]{:S(2)}) async-start(), calls=%async_computation.2 | async-start | bytes 3145728 | tf_op jit(solution)/shard_map/psum | solution.py:9
  10.4 0.7 copy-start.6
  11.1 2.0 slice-start
  17.8 1.0 copy-start.7
  17.8 3.1 copy-start.5
  18.8 285.6 %all-reduce.7.cloned.1.call-start = ((), (), s32[]{:S(2)}) async-start(), calls=%async_computation | async-start | bytes 2097152 | tf_op jit(solution)/shard_map/psum | solution.py:9
  22.0 409.9 %all-reduce.9.cloned.1.call-start = ((), (), s32[]{:S(2)}) async-start(), calls=%async_computation.1 | async-start | bytes 3145728 | tf_op jit(solution)/shard_map/psum | solution.py:9
  146.4 1.6 copy-start.1
  146.4 1.6 copy-start.3
  435.5 1.6 copy-start.2
  435.5 1.6 copy-start.4
  437.2 1.4 copy-start
Sparse Core Ops, SparseCore 0:
  18.9 123.9 all-reduce.10
  146.8 157.4 all-reduce.6
  311.6 120.1 all-reduce.8
where the time goes:
time: 451 us
  waiting for transfers between devices  397 us (88%)
  local copies, waits for them, and re-layouts  26.8 us (6%)
  between operations  14.8 us (3%)
  matrix products  7.36 us (2%)
  other arithmetic  5.39 us (1%)
    psum x3, waiting for transfers between devices, spread(): return lax.psum(block, axis)  397 us
  transfers between devices with their start and end apart: 3, of which 3 were waited for; matrix products, arithmetic and copies ran while one was open for 2% of the time, Pallas kernels for 0%

commit v1 on v0

v1 whole, which is shorter than its diff:
```python
import jax
import jax.numpy as jnp
from jax import lax
from jax.experimental import pallas as pl
from jax.experimental.pallas import tpu as pltpu
from jax.sharding import PartitionSpec as P

MESH = pl.DeviceIdType.MESH
W = 256
KB = 3
NY = 8
SL = 48
HALF = NY * SL
NX, NZ = 4, 8
NQ = NX * NZ
PR = 16
HOLDERS = (30, 31, 0)


def split(x):
    hi = x.astype(jnp.bfloat16)
    return hi, (x - hi.astype(jnp.float32)).astype(jnp.bfloat16)


def dot(a, b, ca, cb):
    return lax.dot_general(a, b, (((ca,), (cb,)), ((), ())), preferred_element_type=jnp.float32)


def kernel(a_hbm, l_hbm, inv_ref, piv_ref, own_ref, o_hbm, a, loc, pt, pair, s_buf, f_buf, b_buf, r_buf, ut, tt, tsrc,
           lp, lg, o_buf, load_sem, out_sem, pair_s, pair_r, rs_s, rs_r, ts_s, ts_r, ag_s, ag_r, fw_s, fw_r,
           sc_s, sc_r, z_s, z_r, x_s, x_r):
    p, q = lax.axis_index("prow"), lax.axis_index("pcol")
    y, c = p // 2, p % 2
    x, z = q // NZ, q % NZ
    side = 1 - 2 * c

    def at_y(step):
        return (lax.rem(y + step + 2 * NY, NY) * 2 + c, q)

    def chip(step):
        return lax.rem(y + step + 2 * NY, NY)

    mate = (y * 2 + 1 - c, q)

    def at_x(step):
        return (p, lax.rem(x + step, NX) * NZ + z)

    def at_z(step):
        return (p, x * NZ + lax.rem(z + step, NZ))

    sent = []

    def send(src, dst, s, r, to):
        copy = pltpu.make_async_remote_copy(src_ref=src, dst_ref=dst, send_sem=s, recv_sem=r, device_id=to,
                                            device_id_type=MESH)
        copy.start()
        sent.append(copy)
        return copy

    load_a = pltpu.make_async_copy(a_hbm, a, load_sem.at[0])
    load_l = pltpu.make_async_copy(l_hbm, loc, load_sem.at[1])
    load_a.start()
    load_l.start()

    barrier = pltpu.get_barrier_semaphore()
    greet = [at_y(i) for i in range(1, NY)] + [mate] + [at_z(i) for i in range(1, NZ)] + [at_x(i) for i in range(1, NX)]
    for to in greet:
        pl.semaphore_signal(barrier, inc=1, device_id=to, device_id_type=MESH)
    for h in HOLDERS:
        @pl.when(q != h)
        def _():
            pl.semaphore_signal(barrier, inc=1, device_id=(p, h), device_id_type=MESH)

    @pl.when(y != 0)
    def _():
        pl.semaphore_signal(barrier, inc=1, device_id=(1 - c, q), device_id_type=MESH)

    def onehot(s, j):
        rows = lax.broadcasted_iota(jnp.int32, (W, W), 0) + (j * 2 * NY + p) * W
        return rows == piv_ref[s:s + 1, :]

    def offer(s):
        hot = [jnp.where(onehot(s, j), 1.0, 0.0).astype(jnp.bfloat16) for j in range(2)]
        for k in range(KB):
            total = jnp.zeros((W, W), jnp.float32)
            for j in range(2):
                for part in split(a[j, k]):
                    total = total + dot(part, hot[j], 0, 0)
            pt[s, k * W:(k + 1) * W, :] = total

    load_a.wait()
    offer(0)

    holds = jnp.logical_or(q == HOLDERS[0], jnp.logical_or(q == HOLDERS[1], q == HOLDERS[2]))
    heard = len(greet) + jnp.where(holds, NQ - 1, 0) + jnp.where(y == 0, NY - 1, 0)
    pl.semaphore_wait(barrier, heard)

    load_l.wait()
    mine = pl.multiple_of(c * HALF, 8)
    other = pl.multiple_of((1 - c) * HALF, 8)

    def rows_of(step):
        return pl.ds(pl.multiple_of(c * HALF + chip(step) * SL, 8), SL)

    def gather_near(buf, i):
        here = buf.at[rows_of(0)]
        return {st: send(here, here, ag_s.at[i, n], ag_r.at[i, n], at_y(st)) for n, st in enumerate((1, -1, 2, -2))}

    def gather_far(buf, i, near):
        far = []
        near[2].wait_recv()
        from_low = buf.at[rows_of(-2)]
        far.append(send(from_low, from_low, ag_s.at[i, 4], ag_r.at[i, 4], at_y(1)))
        near[-2].wait_recv()
        from_high = buf.at[rows_of(2)]
        far.append(send(from_high, from_high, ag_s.at[i, 5], ag_r.at[i, 5], at_y(-1)))
        across = buf.at[rows_of(-2 * side)]
        far.append(send(across, across, ag_s.at[i, 6], ag_r.at[i, 6], at_y(2 * side)))
        return far

    def share(buf, i, near, far):
        moves = []

        def move(n, step):
            piece = buf.at[rows_of(step)]
            moves.append(send(piece, piece, fw_s.at[i, n], fw_r.at[i, n], mate))

        move(0, 0)
        move(1, 2)
        move(2, -2)
        near[1].wait_recv()
        move(3, -1)
        near[-1].wait_recv()
        move(4, 1)
        far[0].wait_recv()
        move(5, -3)
        far[1].wait_recv()
        move(6, 3)
        far[2].wait_recv()
        move(7, 4)
        return moves

    for s in range(2):
        if s == 1:
            offer(1)
        pair_copy = send(pt.at[s, pl.ds(other, HALF)], pair.at[s], pair_s.at[s], pair_r.at[s], mate)

        @pl.when(p == s)
        def _():
            for k in range(KB):
                tsrc[s, k * W:(k + 1) * W, :] = a[0, k].T
            for t in range(2 * NY):
                piece = pl.ds((t % 2) * HALF + (t // 2) * SL, SL)
                if t == s:
                    tt[s, piece, :] = tsrc[s, piece, :]
                else:
                    pltpu.make_async_remote_copy(src_ref=tsrc.at[s, piece], dst_ref=tt.at[s, piece],
                                                 send_sem=ts_s.at[s, t], recv_sem=ts_r.at[s], device_id=(t, q),
                                                 device_id_type=MESH).start()

        if s == 0:
            for n, h in enumerate(HOLDERS):
                @pl.when(q == h)
                def _():
                    lp[n] = loc[h * PR:(h + 1) * PR, :]

                    @pl.loop(1, NQ)
                    def _(i):
                        to = lax.rem(h + i, NQ)
                        piece = pl.ds(pl.multiple_of(to * PR, 8), PR)
                        pltpu.make_async_remote_copy(src_ref=loc.at[piece], dst_ref=lp.at[n], send_sem=sc_s.at[i],
                                                     recv_sem=sc_r.at[n], device_id=(p, to),
                                                     device_id_type=MESH).start()

        pair_copy.wait_recv()
        for i in range(NY):
            s_buf[s, i] = pt[s, pl.ds(pl.multiple_of(mine + i * SL, 8), SL), :] + pair[s, i * SL:(i + 1) * SL, :]

        far = [
            send(s_buf.at[s, chip(-3)], f_buf.at[s, 0], rs_s.at[s, 0], rs_r.at[s, 0], at_y(-1)),
            send(s_buf.at[s, chip(4)], f_buf.at[s, 1], rs_s.at[s, 1], rs_r.at[s, 1], at_y(-2 * side)),
            send(s_buf.at[s, chip(3)], f_buf.at[s, 2], rs_s.at[s, 2], rs_r.at[s, 2], at_y(1)),
        ]
        near = [
            send(s_buf.at[s, chip(1)], r_buf.at[s, 0], rs_s.at[s, 3], rs_r.at[s, 3], at_y(1)),
            send(s_buf.at[s, chip(-1)], r_buf.at[s, 1], rs_s.at[s, 4], rs_r.at[s, 4], at_y(-1)),
        ]
        for copy in far:
            copy.wait_recv()
        cross = f_buf[s, 1]
        b_buf[s, 0] = s_buf[s, chip(-2)] + f_buf[s, 0] + jnp.where(c == 0, cross, 0.0)
        b_buf[s, 1] = s_buf[s, chip(2)] + f_buf[s, 2] + jnp.where(c == 0, 0.0, cross)
        near += [
            send(b_buf.at[s, 0], r_buf.at[s, 2], rs_s.at[s, 5], rs_r.at[s, 5], at_y(-2)),
            send(b_buf.at[s, 1], r_buf.at[s, 3], rs_s.at[s, 6], rs_r.at[s, 6], at_y(2)),
        ]

        t_here = tt.at[s, rows_of(0)]

        @pl.when(p != s)
        def _():
            pltpu.make_async_remote_copy(src_ref=t_here, dst_ref=t_here, send_sem=ts_s.at[s, 0], recv_sem=ts_r.at[s],
                                         device_id=mate, device_id_type=MESH).wait_recv()
        t_near = gather_near(tt.at[s], 2 * s)

        if s == 0:
            for n, h in enumerate(HOLDERS):
                @pl.when(q != h)
                def _():
                    pltpu.make_async_remote_copy(src_ref=lp.at[n], dst_ref=lp.at[n], send_sem=sc_s.at[0],
                                                 recv_sem=sc_r.at[n], device_id=mate, device_id_type=MESH).wait_recv()
            piece = pl.ds(pl.multiple_of(q * PR, 8), PR)
            for i in range(2):
                chosen = jnp.where(own_ref[i] == HOLDERS[1], lp[1], jnp.where(own_ref[i] == HOLDERS[0], lp[0], lp[2]))
                lg[i, piece, :] = chosen
            z_copies = [send(lg.at[:, piece], lg.at[:, piece], z_s.at[i], z_r.at[i], at_z(i)) for i in range(1, NZ)]

        for copy in near:
            copy.wait_recv()
        total = s_buf[s, y] + r_buf[s, 0] + r_buf[s, 1] + r_buf[s, 2] + r_buf[s, 3]
        ut[s, rows_of(0), :] = lax.dot_general(total, inv_ref[s], (((1,), (1,)), ((), ())),
                                               precision=lax.Precision.HIGHEST, preferred_element_type=jnp.float32)
        u_near = gather_near(ut.at[s], 2 * s + 1)
        t_far = gather_far(tt.at[s], 2 * s, t_near)

        if s == 0:
            for copy in z_copies:
                copy.wait_recv()
            wide = pl.ds(pl.multiple_of(x * (NZ * PR), 8), NZ * PR)
            x_copies = [[send(lg.at[i, wide], lg.at[i, wide], x_s.at[i, n], x_r.at[i, n], at_x(n))
                         for n in range(1, NX)] for i in range(2)]

        u_far = gather_far(ut.at[s], 2 * s + 1, u_near)
        moves = share(tt.at[s], 2 * s, t_near, t_far)
        moves += share(ut.at[s], 2 * s + 1, u_near, u_far)
        for copy in moves:
            copy.wait_recv()
        for copy in x_copies[s]:
            copy.wait_recv()

        hot = [onehot(s, j) for j in range(2)]
        taken = [jnp.sum(jnp.where(h, 1.0, 0.0), axis=1, keepdims=True) > 0.0 for h in hot]
        hot = [jnp.where(h, 1.0, 0.0).astype(jnp.bfloat16) for h in hot]
        low = [jnp.where(p > s, lg[s, :W, :], 0.0), lg[s, W:, :]]
        low = [split(v) for v in low]
        out = a if s == 0 else o_buf
        for k in range(KB):
            cols = pl.ds(k * W, W)
            t_parts = split(tt[s, cols, :])
            u_parts = split(ut[s, cols, :])
            for j in range(2):
                swapped = dot(hot[j], t_parts[0], 1, 1) + dot(hot[j], t_parts[1], 1, 1)
                base = jnp.where(taken[j], swapped, a[j, k])
                product = (dot(low[j][0], u_parts[0], 1, 1) + dot(low[j][0], u_parts[1], 1, 1)
                           + dot(low[j][1], u_parts[0], 1, 1))
                out[j, k] = base - product

        @pl.when(p == s)
        def _():
            for k in range(KB):
                out[0, k] = ut[s, k * W:(k + 1) * W, :].T

    store = pltpu.make_async_copy(o_buf, o_hbm, out_sem)
    store.start()
    for copy in sent:
        copy.wait_send()
    for s in range(2):
        @pl.when(p == s)
        def _():
            for t in range(2 * NY):
                if t != s:
                    piece = pl.ds((t % 2) * HALF + (t // 2) * SL, SL)
                    pltpu.make_async_remote_copy(src_ref=tsrc.at[s, piece], dst_ref=tt.at[s, piece],
                                                 send_sem=ts_s.at[s, t], recv_sem=ts_r.at[s], device_id=(t, q),
                                                 device_id_type=MESH).wait_send()
    for n, h in enumerate(HOLDERS):
        @pl.when(q == h)
        def _():
            @pl.loop(1, NQ)
            def _(i):
                piece = pl.ds(0, PR)
                pltpu.make_async_remote_copy(src_ref=loc.at[piece], dst_ref=lp.at[n], send_sem=sc_s.at[i],
                                             recv_sem=sc_r.at[n], device_id=mate, device_id_type=MESH).wait_send()
    store.wait()


def body(matrix, lower_panel, inverses, pivots, panel_owner):
    f32 = jnp.float32
    dma = pltpu.SemaphoreType.DMA
    blocks = matrix.transpose(0, 2, 1, 3)
    any_spec = pl.BlockSpec(memory_space=pl.ANY)
    vmem = pl.BlockSpec(memory_space=pltpu.VMEM)
    line = KB * W
    out = pl.pallas_call(
        kernel,
        out_shape=jax.ShapeDtypeStruct(blocks.shape, f32),
        in_specs=[any_spec, any_spec, vmem, vmem, pl.BlockSpec(memory_space=pltpu.SMEM)],
        out_specs=any_spec,
        scratch_shapes=[
            pltpu.VMEM((2, KB, W, W), f32),
            pltpu.VMEM((2 * W, W), f32),
            pltpu.VMEM((2, line, W), f32),
            pltpu.VMEM((2, HALF, W), f32),
            pltpu.VMEM((2, NY, SL, W), f32),
            pltpu.VMEM((2, 3, SL, W), f32),
            pltpu.VMEM((2, 2, SL, W), f32),
            pltpu.VMEM((2, 4, SL, W), f32),
            pltpu.VMEM((2, line, W), f32),
            pltpu.VMEM((2, line, W), f32),
            pltpu.VMEM((2, line, W), f32),
            pltpu.VMEM((3, PR, W), f32),
            pltpu.VMEM((2, 2 * W, W), f32),
            pltpu.VMEM((2, KB, W, W), f32),
            dma((2,)), dma(()),
            dma((2,)), dma((2,)),
            dma((2, 7)), dma((2, 7)),
            dma((2, 2 * NY)), dma((2,)),
            dma((4, 7)), dma((4, 7)),
            dma((4, 8)), dma((4, 8)),
            dma((NQ,)), dma((3,)),
            dma((NZ,)), dma((NZ,)),
            dma((2, NX)), dma((2, NX)),
        ],
        compiler_params=pltpu.CompilerParams(collective_id=0, has_side_effects=True, vmem_limit_bytes=48 * 2**20),
    )(blocks, lower_panel.reshape(2 * W, W), inverses, pivots, panel_owner)
    return out.transpose(0, 2, 1, 3)


def solution(mesh):
    in_specs = (P(None, "prow", None, "pcol"), P(None, "prow", "pcol"), P(), P(), P())
    return jax.shard_map(body, mesh=mesh, in_specs=in_specs, out_specs=P(None, "prow", None, "pcol"), check_vma=False)
```

time: 451 us -> 82.3 us (0.18)
  waiting for transfers between devices: 397 us -> 0 us
  Pallas kernels: 0 us -> 76 us
  local copies, waits for them, and re-layouts: 26.8 us -> 5.97 us
  between operations: 14.8 us -> 0.01 us
  matrix products: 7.36 us -> 0 us
  other arithmetic: 5.39 us -> 0 us
    psum x3 -> x0, waiting for transfers between devices: 397 us -> none  [spread(): return lax.psum(block, axis)]
    pallas_call x0 -> x1, Pallas kernels: none -> 76 us  [body(): pl.pallas_call(kernel, out_shape=jax.ShapeDtypeStruct(blocks.shape, f32),...]
    scatter x5 -> x0, local copies, waits for them, and re-layouts: 8.1 us -> none  [the longest x4 7.64 us: body(): current = current.at[landing].set(top_block, mode='drop')]
    dot_general x4 -> x0, matrix products: 7.36 us -> none  [the longest x2 5.73 us: body(): current = current - jnp.dot(masked, upper, precision=lax.Precision.HIGHEST)]
    reshape x3 -> x0, local copies, waits for them, and re-layouts: 6.92 us -> none  [the longest x1 3.83 us: body(): current = matrix.reshape(row_count, col_count)]
    select_n x9 -> x0, other arithmetic: 5.14 us -> none  [the longest x3 3.22 us: spread(): jnp.where(lax.axis_index(axis) == holder, block, jnp.zeros_like(block))]
    gather x4 -> x0, local copies, waits for them, and re-layouts: 4.71 us -> none  [body(): offered = jnp.where(owned[:, None], current[safe_rows], 0.0)]
  transfers between devices with their start and end apart: 3 -> 0, of which waited for: 3 -> 0; matrix products, arithmetic and copies ran while one was open for 2% -> 0% of each run, Pallas kernels for 0% -> 0%
where the time goes in v1:
time: 82.3 us; the launch traced here: 82 us
  Pallas kernels  76 us (92%)
  local copies, waits for them, and re-layouts  5.97 us (7%)
    pallas_call x1, Pallas kernels, body(): pl.pallas_call(kernel, out_shape=jax.ShapeDtypeStruct(blocks.shape, f32),...  76 us
    unnamed x11, local copies, waits for them, and re-layouts  5.97 us

profile of v1, /device:TPU:1, one launch (start us, length us, event | category | flops | bytes accessed | tf_op | source)
XLA Modules:
  0.0 82.0 jit_solution(4563666570254230884)
XLA Ops:
  0.0 0.0 copy-start
  0.0 1.4 %copy-done = f32[2,256,3,256]{3,1,2,0:T(8,128)S(1)} copy-done((f32[2,256,3,256]{3,1,2,0:T(8,128)S(1)}, f32[2,256,3,256]{3,1,2,0:T(8,128)}, u32[]{:S(2)}) %copy-start) | copy-done | bytes 1572888
  1.4 0.0 copy-start.1
  1.4 1.0 %copy-done.1 = f32[2,256,256]{2,1,0:T(8,128)S(1)} copy-done((f32[2,256,256]{2,1,0:T(8,128)S(1)}, f32[2,256,256]{2,1,0:T(8,128)}, u32[]{:S(2)}) %copy-start.1) | copy-done | bytes 524312
  2.5 0.0 copy-start.2
  2.5 1.0 %copy-done.2 = f32[2,256,256]{2,1,0:T(8,128)S(1)} copy-done((f32[2,256,256]{2,1,0:T(8,128)S(1)}, f32[2,256,256]{2,1,0:T(8,128)}, u32[]{:S(2)}) %copy-start.2) | copy-done | bytes 524312
  3.5 0.0 copy-start.3
  3.5 0.7 copy-done.3
  4.2 0.0 copy-start.4
  4.2 0.7 copy-done.4
  4.8 76.0 %shard_map.55 = f32[2,3,256,256]{3,2,1,0:T(8,128)S(1)} custom-call(f32[2,3,256,256]{3,2,1,0:T(8,128)S(1)} %bitcast.4, f32[512,256]{1,0:T(8,128)S(1)} %bitcast.5, f32[2,256,256]{2,1,0:T(8,128)S(1)} %copy-done.2, s32[2,256]{1,0:T(2,128)S(1)} %copy-done.3, s32[2]{0:T(128)S(1)} %copy-done.4), custom_call_target="tpu_custom_call" | custom-call | tf_op jit(solution)/shard_map/pallas_call | solution.py:294
  80.9 1.1 %copy.7 = f32[2,256,3,256]{3,1,2,0:T(8,128)} copy(f32[2,256,3,256]{3,1,2,0:T(8,128)S(1)} %bitcast.3) | data formatting | bytes 3145728
Async XLA Ops:
  0.0 1.4 %copy-start = (f32[2,256,3,256]{3,1,2,0:T(8,128)S(1)}, f32[2,256,3,256]{3,1,2,0:T(8,128)}, u32[]{:S(2)}) copy-start(f32[2,256,3,256]{3,1,2,0:T(8,128)} %param.5) | copy-start | bytes 4718596
  1.4 1.0 %copy-start.1 = (f32[2,256,256]{2,1,0:T(8,128)S(1)}, f32[2,256,256]{2,1,0:T(8,128)}, u32[]{:S(2)}) copy-start(f32[2,256,256]{2,1,0:T(8,128)} %param.6) | copy-start | bytes 1572868
  2.5 1.0 %copy-start.2 = (f32[2,256,256]{2,1,0:T(8,128)S(1)}, f32[2,256,256]{2,1,0:T(8,128)}, u32[]{:S(2)}) copy-start(f32[2,256,256]{2,1,0:T(8,128)} %inv_ref.1) | copy-start | bytes 1572868
  3.5 0.7 copy-start.3
  4.2 0.7 copy-start.4

commit v2 on v1

--- a/solution.py
+++ b/solution.py
@@ -26,7 +26,7 @@
     return lax.dot_general(a, b, (((ca,), (cb,)), ((), ())), preferred_element_type=jnp.float32)
 
 
-def kernel(a_hbm, l_hbm, inv_ref, piv_ref, own_ref, o_hbm, a, loc, pt, pair, s_buf, f_buf, b_buf, r_buf, ut, tt, tsrc,
+def kernel(a_hbm, l_hbm, inv_hbm, piv_hbm, own_hbm, o_hbm, a, loc, inv_ref, piv_ref, own_ref, pt, pair, s_buf, f_buf, b_buf, r_buf, ut, tt, tsrc,
            lp, lg, o_buf, load_sem, out_sem, pair_s, pair_r, rs_s, rs_r, ts_s, ts_r, ag_s, ag_r, fw_s, fw_r,
            sc_s, sc_r, z_s, z_r, x_s, x_r):
     p, q = lax.axis_index("prow"), lax.axis_index("pcol")
@@ -58,9 +58,11 @@
         return copy
 
     load_a = pltpu.make_async_copy(a_hbm, a, load_sem.at[0])
-    load_l = pltpu.make_async_copy(l_hbm, loc, load_sem.at[1])
-    load_a.start()
-    load_l.start()
+    load_p = pltpu.make_async_copy(piv_hbm, piv_ref, load_sem.at[1])
+    load_rest = [pltpu.make_async_copy(src, dst, load_sem.at[2 + i]) for i, (src, dst) in enumerate(
+        ((l_hbm, loc), (inv_hbm, inv_ref), (own_hbm, own_ref)))]
+    for copy in [load_p, load_a] + load_rest:
+        copy.start()
 
     barrier = pltpu.get_barrier_semaphore()
     greet = [at_y(i) for i in range(1, NY)] + [mate] + [at_z(i) for i in range(1, NZ)] + [at_x(i) for i in range(1, NX)]
@@ -88,6 +90,7 @@
                     total = total + dot(part, hot[j], 0, 0)
             pt[s, k * W:(k + 1) * W, :] = total
 
+    load_p.wait()
     load_a.wait()
     offer(0)
 
@@ -95,7 +98,8 @@
     heard = len(greet) + jnp.where(holds, NQ - 1, 0) + jnp.where(y == 0, NY - 1, 0)
     pl.semaphore_wait(barrier, heard)
 
-    load_l.wait()
+    for copy in load_rest:
+        copy.wait()
     mine = pl.multiple_of(c * HALF, 8)
     other = pl.multiple_of((1 - c) * HALF, 8)
 
@@ -289,16 +293,18 @@
     dma = pltpu.SemaphoreType.DMA
     blocks = matrix.transpose(0, 2, 1, 3)
     any_spec = pl.BlockSpec(memory_space=pl.ANY)
-    vmem = pl.BlockSpec(memory_space=pltpu.VMEM)
     line = KB * W
     out = pl.pallas_call(
         kernel,
         out_shape=jax.ShapeDtypeStruct(blocks.shape, f32),
-        in_specs=[any_spec, any_spec, vmem, vmem, pl.BlockSpec(memory_space=pltpu.SMEM)],
+        in_specs=[any_spec] * 5,
         out_specs=any_spec,
         scratch_shapes=[
             pltpu.VMEM((2, KB, W, W), f32),
             pltpu.VMEM((2 * W, W), f32),
+            pltpu.VMEM((2, W, W), f32),
+            pltpu.VMEM((2, W), jnp.int32),
+            pltpu.SMEM((2,), jnp.int32),
             pltpu.VMEM((2, line, W), f32),
             pltpu.VMEM((2, HALF, W), f32),
             pltpu.VMEM((2, NY, SL, W), f32),
@@ -311,7 +317,7 @@
             pltpu.VMEM((3, PR, W), f32),
             pltpu.VMEM((2, 2 * W, W), f32),
             pltpu.VMEM((2, KB, W, W), f32),
-            dma((2,)), dma(()),
+            dma((5,)), dma(()),
             dma((2,)), dma((2,)),
             dma((2, 7)), dma((2, 7)),
             dma((2, 2 * NY)), dma((2,)),
@@ -321,7 +327,7 @@
             dma((NZ,)), dma((NZ,)),
             dma((2, NX)), dma((2, NX)),
         ],
-        compiler_params=pltpu.CompilerParams(collective_id=0, has_side_effects=True, vmem_limit_bytes=48 * 2**20),
+        compiler_params=pltpu.CompilerParams(collective_id=0, has_side_effects=True, vmem_limit_bytes=60 * 2**20),
     )(blocks, lower_panel.reshape(2 * W, W), inverses, pivots, panel_owner)
     return out.transpose(0, 2, 1, 3)
 

time: 82.3 us -> 77.1 us (0.937)
  local copies, waits for them, and re-layouts: 5.97 us -> 2.74 us
  Pallas kernels: 76 us -> 74.2 us
    unnamed x11 -> x1, local copies, waits for them, and re-layouts: 5.97 us -> 2.74 us
    pallas_call x1, Pallas kernels: 76 us -> 74.2 us  [body(): pl.pallas_call(kernel, out_shape=jax.ShapeDtypeStruct(blocks.shape, f32),...]
where the time goes in v2:
time: 77.1 us; the launch traced here: 76.9 us
  Pallas kernels  74.2 us (96%)
  local copies, waits for them, and re-layouts  2.74 us (4%)
    pallas_call x1, Pallas kernels, body(): pl.pallas_call(kernel, out_shape=jax.ShapeDtypeStruct(blocks.shape, f32),...  74.2 us
    unnamed x1, local copies, waits for them, and re-layouts  2.74 us

profile of v2, /device:TPU:1, one launch (start us, length us, event | category | flops | bytes accessed | tf_op | source)
XLA Modules:
  0.0 76.9 jit_solution(8153983669631304589)
XLA Ops:
  0.0 74.2 %shard_map.55 = f32[2,3,256,256]{3,2,1,0:T(8,128)} custom-call(f32[2,3,256,256]{3,2,1,0:T(8,128)} %bitcast.4, f32[512,256]{1,0:T(8,128)} %bitcast.5, f32[2,256,256]{2,1,0:T(8,128)} %inv_hbm.1, s32[2,256]{1,0:T(2,128)} %piv_hbm.1, s32[2]{0:T(128)} %own_hbm.1), custom_call_target="tpu_custom_call" | custom-call | tf_op jit(solution)/shard_map/pallas_call | solution.py:297
  74.2 2.7 %copy.7 = f32[2,256,3,256]{3,1,2,0:T(8,128)} copy(f32[2,256,3,256]{3,1,2,0:T(8,128)} %bitcast.3) | data formatting | bytes 3145728

commit v3 on v0

v3 whole, which is shorter than its diff:
```python
import jax
import jax.numpy as jnp
from jax import lax
from jax.experimental import pallas as pl
from jax.experimental.pallas import tpu as pltpu
from jax.sharding import PartitionSpec as P

MESH = pl.DeviceIdType.MESH
W = 256
KB = 3
NY = 8
ST = 2
SL = 24
WIDE = 2 * NY * SL
NX, NZ = 4, 8
NQ = NX * NZ
PR = 16
HOLDERS = (30, 31, 0)


def split(x):
    hi = x.astype(jnp.bfloat16)
    return hi, (x - hi.astype(jnp.float32)).astype(jnp.bfloat16)


def dot(a, b, ca, cb):
    return lax.dot_general(a, b, (((ca,), (cb,)), ((), ())), preferred_element_type=jnp.float32)


def dot3(a, b):
    return dot(a[0], b[0], 1, 1) + dot(a[0], b[1], 1, 1) + dot(a[1], b[0], 1, 1)


def as_hot(mask):
    return jnp.where(mask, 1.0, 0.0).astype(jnp.bfloat16)


def kernel(a_hbm, l_hbm, inv_hbm, piv_hbm, own_hbm, o_hbm, a, loc, inv_ref, piv_ref, own_ref, pt, pair, s_buf, f_buf,
           b_buf, g_buf, d_buf, r_buf, ut, tt, tsrc, lp, lg, et, ep, es, er, ms, mr, mn, t1, u1, o_buf, load_sem, out_sem, pair_s,
           pair_r, rs_s, rs_r, ts_s, ts_r, ag_s, ag_r, fw_s, fw_r, sc_s, sc_r, z_s, z_r, x_s, x_r, e_s, e_r, n_s, n_r,
           m_s, m_r):
    p, q = lax.axis_index("prow"), lax.axis_index("pcol")
    y, c = p // 2, p % 2
    x, z = q // NZ, q % NZ
    side = 1 - 2 * c

    def chip(step):
        return lax.rem(y + step + 2 * NY, NY)

    def at_y(step):
        return (chip(step) * 2 + c, q)

    mate = (y * 2 + 1 - c, q)

    def at_x(step):
        return (p, lax.rem(x + step, NX) * NZ + z)

    def at_z(step):
        return (p, x * NZ + lax.rem(z + step, NZ))

    sent = []

    def remote(src, dst, s, r, to):
        return pltpu.make_async_remote_copy(src_ref=src, dst_ref=dst, send_sem=s, recv_sem=r, device_id=to,
                                            device_id_type=MESH)

    def send(src, dst, s, r, to):
        copy = remote(src, dst, s, r, to)
        copy.start()
        sent.append(copy)
        return copy

    def settle(copies):
        for copy in copies:
            copy.wait_recv()

    load_a = pltpu.make_async_copy(a_hbm, a, load_sem.at[0])
    load_p = pltpu.make_async_copy(piv_hbm, piv_ref, load_sem.at[1])
    load_rest = [pltpu.make_async_copy(src, dst, load_sem.at[2 + i]) for i, (src, dst) in enumerate(
        ((l_hbm, loc), (inv_hbm, inv_ref), (own_hbm, own_ref)))]
    for copy in [load_p, load_a] + load_rest:
        copy.start()

    barrier = pltpu.get_barrier_semaphore()
    for h in HOLDERS:
        @pl.when(q != h)
        def _():
            pl.semaphore_signal(barrier, inc=1, device_id=(p, h), device_id_type=MESH)
    greet = [at_y(i) for i in range(1, NY)] + [mate] + [at_z(i) for i in range(1, NZ)] + [at_x(i) for i in range(1, NX)]
    for to in greet:
        pl.semaphore_signal(barrier, inc=1, device_id=to, device_id_type=MESH)

    @pl.when(y != 0)
    def _():
        pl.semaphore_signal(barrier, inc=1, device_id=(1 - c, q), device_id_type=MESH)

    def onehot(j, wanted):
        rows = lax.broadcasted_iota(jnp.int32, (W, W), 0) + (j * 2 * NY + p) * W
        return rows == wanted

    def pick(wanted):
        hot = [as_hot(onehot(j, wanted)) for j in range(2)]
        blocks = []
        for k in range(KB):
            total = jnp.zeros((W, W), jnp.float32)
            for j in range(2):
                for part in split(a[j, k]):
                    total = total + dot(part, hot[j], 0, 0)
            blocks.append(total)
        return jnp.concatenate(blocks, axis=0).reshape(ST, 2, NY, SL, W)

    load_p.wait()
    load_a.wait()
    pt[0] = pick(piv_ref[0:1, :])

    holds = jnp.logical_or(q == HOLDERS[0], jnp.logical_or(q == HOLDERS[1], q == HOLDERS[2]))
    heard = len(greet) + jnp.where(holds, NQ - 1, 0) + jnp.where(y == 0, NY - 1, 0)
    pl.semaphore_wait(barrier, heard)

    for copy in load_rest:
        copy.wait()

    def scatter(n):
        h = HOLDERS[n]

        @pl.when(q == h)
        def _():
            lp[n] = loc[h * PR:(h + 1) * PR, :]

            @pl.loop(1, NQ)
            def _(i):
                to = lax.rem(h + i, NQ)
                piece = pl.ds(pl.multiple_of(to * PR, 8), PR)
                pltpu.make_async_remote_copy(src_ref=loc.at[piece], dst_ref=lp.at[n], send_sem=sc_s.at[i],
                                             recv_sem=sc_r.at[n], device_id=(p, to), device_id_type=MESH).start()

    def arrived(n):
        @pl.when(q != HOLDERS[n])
        def _():
            pltpu.make_async_remote_copy(src_ref=lp.at[n], dst_ref=lp.at[n], send_sem=sc_s.at[0],
                                         recv_sem=sc_r.at[n], device_id=mate, device_id_type=MESH).wait_recv()

    l_rows = pl.ds(pl.multiple_of(q * PR, 8), PR)
    l_wide = pl.ds(pl.multiple_of(x * (NZ * PR), 8), NZ * PR)

    def gather_z(i):
        lg[i, l_rows, :] = jnp.where(own_ref[i] == HOLDERS[1], lp[1], lp[2 * i])
        piece = lg.at[i, l_rows]
        return [send(piece, piece, z_s.at[i, n], z_r.at[i, n], at_z(n)) for n in range(1, NZ)]

    def gather_x(i):
        piece = lg.at[i, l_wide]
        return [send(piece, piece, x_s.at[i, n], x_r.at[i, n], at_x(n)) for n in range(1, NX)]

    def pair_up(s, h):
        return send(pt.at[s, h, 1 - c], pair.at[s, h], pair_s.at[s, h], pair_r.at[s, h], mate)

    def reduce_first(s, h, pair_copy):
        pair_copy.wait_recv()
        s_buf[s, h] = pt[s, h, c] + pair[s, h]
        plan = ((-3, -1), (4, -2 * side), (3, 1))
        return [send(s_buf.at[s, h, chip(end)], f_buf.at[s, h, n], rs_s.at[s, h, n], rs_r.at[s, h, n], at_y(to))
                for n, (end, to) in enumerate(plan)]

    def reduce_second(s, h, first):
        settle(first)
        cross = f_buf[s, h, 1]
        b_buf[s, h, 0] = s_buf[s, h, chip(-2)] + f_buf[s, h, 0] + jnp.where(c == 0, cross, 0.0)
        b_buf[s, h, 1] = s_buf[s, h, chip(2)] + f_buf[s, h, 2] + jnp.where(c == 0, 0.0, cross)
        return [send(b_buf.at[s, h, n], g_buf.at[s, h, n], rs_s.at[s, h, 3 + n], rs_r.at[s, h, 3 + n], at_y(to))
                for n, to in enumerate((-1, 1))]

    def reduce_third(s, h, second):
        settle(second)
        d_buf[s, h, 0] = s_buf[s, h, chip(-1)] + g_buf[s, h, 0]
        d_buf[s, h, 1] = s_buf[s, h, chip(1)] + g_buf[s, h, 1]
        return [send(d_buf.at[s, h, n], r_buf.at[s, h, n], rs_s.at[s, h, 5 + n], rs_r.at[s, h, 5 + n], at_y(to))
                for n, to in enumerate((-1, 1))]

    def solve(s, h, last):
        settle(last)
        total = s_buf[s, h, y] + r_buf[s, h, 0] + r_buf[s, h, 1]
        ut[s, h, c, y] = lax.dot_general(total, inv_ref[s], (((1,), (1,)), ((), ())),
                                         precision=lax.Precision.HIGHEST, preferred_element_type=jnp.float32)

    def upper_piece(s, h):
        return lambda step: ut.at[s, h, c, chip(step)]

    def top_piece(s):
        return lambda step: tt.at[s, :, c, chip(step)]

    def gather_first(piece, i):
        return [send(piece(0), piece(0), ag_s.at[i, n], ag_r.at[i, n], at_y(to)) for n, to in enumerate((1, -1))]

    def gather_second(piece, i, first):
        copies = []
        for n, to in enumerate((1, -1)):
            first[n].wait_recv()
            copies.append(send(piece(-to), piece(-to), ag_s.at[i, 2 + n], ag_r.at[i, 2 + n], at_y(to)))
        return copies

    def gather_third(piece, i, second):
        copies = []
        for n, to in enumerate((1, -1)):
            second[n].wait_recv()
            copies.append(send(piece(-2 * to), piece(-2 * to), ag_s.at[i, 4 + n], ag_r.at[i, 4 + n], at_y(to)))
        over = piece(-2 * side)
        return copies + [send(over, over, ag_s.at[i, 6], ag_r.at[i, 6], at_y(2 * side))]

    def share(half, i, far):
        settle(far)
        return send(half, half, fw_s.at[i], fw_r.at[i], mate)

    def spread_top(s):
        @pl.when(p == s)
        def _():
            tsrc[s] = jnp.concatenate([a[0, k].T for k in range(KB)], axis=0).reshape(ST, 2, NY, SL, W)
            for t in range(2 * NY):
                src, dst = tsrc.at[s, :, t % 2, t // 2], tt.at[s, :, t % 2, t // 2]
                if t == s:
                    tt[s, :, t % 2, t // 2] = tsrc[s, :, t % 2, t // 2]
                else:
                    pltpu.make_async_remote_copy(src_ref=src, dst_ref=dst, send_sem=ts_s.at[s, t], recv_sem=ts_r.at[s],
                                                 device_id=(t, q), device_id_type=MESH).start()

    def gather_top(s):
        here = tt.at[s, :, c, y]

        @pl.when(p != s)
        def _():
            pltpu.make_async_remote_copy(src_ref=here, dst_ref=here, send_sem=ts_s.at[s, 0], recv_sem=ts_r.at[s],
                                         device_id=mate, device_id_type=MESH).wait_recv()
        return gather_first(top_piece(s), 3 * s + 2)

    def swap(s, j, tops):
        mask = onehot(j, piv_ref[s:s + 1, :])
        taken = jnp.sum(jnp.where(mask, 1.0, 0.0), axis=1, keepdims=True) > 0.0
        hot = as_hot(mask)
        new = []
        for k in range(KB):
            hi, lo = split(tops[k * W:(k + 1) * W])
            new.append(jnp.where(taken, dot(hot, hi, 1, 1) + dot(hot, lo, 1, 1), a[j, k]))
        return new

    def below(s, j):
        return split(lg[s, W:, :] if j else jnp.where(p > s, lg[s, :W, :], 0.0))

    def update(j):
        new = swap(0, j, tt[0].reshape(KB * W, W))
        low = below(0, j)
        upper = ut[0].reshape(KB * W, W)
        for k in range(KB):
            a[j, k] = new[k] - dot3(low, split(upper[k * W:(k + 1) * W]))

    lined = jnp.logical_or(q == HOLDERS[0], q == HOLDERS[1])

    def rows_first():
        @pl.when(lined)
        def _():
            hot = [as_hot(onehot(j, piv_ref[1:2, :])) for j in range(2)]
            total = jnp.zeros((W, W), jnp.float32)
            for j in range(2):
                for part in split(loc[j * W:(j + 1) * W, :]):
                    total = total + dot(hot[j], part, 0, 0)
            et[...] = total.reshape(2, NY, PR, W)
            remote(et.at[1 - c], ep, e_s.at[0], e_r.at[0], mate).start()

            @pl.when(p == 1)
            def _():
                for t in range(2 * NY):
                    piece = pl.ds((t % 2) * NY * PR + (t // 2) * PR, PR)
                    if t == 1:
                        ms[1] = loc[piece, :]
                    else:
                        remote(loc.at[piece], ms.at[1], n_s.at[t], n_r, (t, q)).start()

    def rows_second():
        @pl.when(lined)
        def _():
            remote(et.at[1 - c], ep, e_s.at[0], e_r.at[0], mate).wait_recv()
            es[...] = et[c] + ep[...]
            for i in range(1, NY):
                remote(es.at[chip(i)], er.at[i - 1], e_s.at[i], e_r.at[i], at_y(i)).start()

    def rows_third():
        @pl.when(lined)
        def _():
            total = es[y]
            for i in range(1, NY):
                remote(es.at[chip(i)], er.at[i - 1], e_s.at[i], e_r.at[i], at_y(i)).wait_recv()
                total = total + er[i - 1]
            ms[0] = total

            @pl.when(p != 1)
            def _():
                remote(ms.at[1], ms.at[1], n_s.at[0], n_r, mate).wait_recv()
        for n in range(2):
            @pl.when(q == HOLDERS[n])
            def _():
                mr[n] = ms[...]
                for i in range(1, NX):
                    remote(mr.at[n], mr.at[n], m_s.at[i], m_r.at[n], at_x(i)).start()

    def rows_fourth():
        for n in range(2):
            @pl.when(z == HOLDERS[n] % NZ)
            def _():
                @pl.when(q != HOLDERS[n])
                def _():
                    remote(mr.at[n], mr.at[n], m_s.at[0], m_r.at[n], mate).wait_recv()
                for i in range(1, NZ):
                    remote(mr.at[n], mr.at[n], m_s.at[NX + i], m_r.at[n], at_z(i)).start()

    def rows_here():
        for n in range(2):
            @pl.when(z != HOLDERS[n] % NZ)
            def _():
                remote(mr.at[n], mr.at[n], m_s.at[0], m_r.at[n], mate).wait_recv()
        mn[:, c, y] = jnp.where(own_ref[0] == HOLDERS[0], mr[0], mr[1])

    def rows_piece(step):
        return mn.at[:, c, chip(step)]

    every = [(s, h) for s in range(2) for h in range(ST)]
    slot = {(s, h): 3 * s + h for s, h in every}

    pairs = {(0, h): pair_up(0, h) for h in range(ST)}
    rows_first()

    first = jnp.broadcast_to(piv_ref[0:1, :].astype(jnp.float32), (W, W)).T
    hit = jnp.where(first == piv_ref[1:2, :].astype(jnp.float32), 1.0, 0.0)
    place = jnp.sum(hit * lax.broadcasted_iota(jnp.int32, (W, W), 0).astype(jnp.float32), axis=0, keepdims=True)
    moved = jnp.sum(hit, axis=0, keepdims=True) > 0.0
    pt[1] = pick(jnp.where(moved, place.astype(jnp.int32), piv_ref[1:2, :]))
    pairs.update({(1, h): pair_up(1, h) for h in range(ST)})

    work = {k: reduce_first(*k, pairs[k]) for k in every}
    rows_second()
    for n in range(len(HOLDERS)):
        scatter(n)
    for s in range(2):
        spread_top(s)
    work = {k: reduce_second(*k, work[k]) for k in every}
    rows_third()
    for n in range(len(HOLDERS)):
        arrived(n)
    z_copies = [gather_z(i) for i in range(2)]
    work = {k: reduce_third(*k, work[k]) for k in every}
    rows_fourth()
    upper = {}
    for k in every:
        solve(*k, work[k])
        upper[k] = gather_first(upper_piece(*k), slot[k])
    tops = [gather_top(s) for s in range(2)]
    x_copies = []
    for i in range(2):
        settle(z_copies[i])
        x_copies.append(gather_x(i))
    upper = {k: gather_second(upper_piece(*k), slot[k], upper[k]) for k in every}
    tops = [gather_second(top_piece(s), 3 * s + 2, tops[s]) for s in range(2)]
    rows_here()
    rows = gather_first(rows_piece, 6)
    upper = {k: gather_third(upper_piece(*k), slot[k], upper[k]) for k in every}
    tops = [gather_third(top_piece(s), 3 * s + 2, tops[s]) for s in range(2)]
    rows = gather_second(rows_piece, 6, rows)
    upper = {k: share(ut.at[k[0], k[1], c], slot[k], upper[k]) for k in every}
    rows = gather_third(rows_piece, 6, rows)
    tops = [share(tt.at[s, :, c], 3 * s + 2, tops[s]) for s in range(2)]
    rows = share(mn.at[:, c], 6, rows)

    settle(tops)
    settle(x_copies[0])
    for h in range(ST):
        upper[0, h].wait_recv()
    for j in range(2):
        update(j)

    @pl.when(p == 0)
    def _():
        whole = ut[0].reshape(KB * W, W)
        for k in range(KB):
            a[0, k] = whole[k * W:(k + 1) * W].T

    rows.wait_recv()
    solved = [split(ut[0, h].reshape(WIDE, W)) for h in range(ST)]
    ids = lax.broadcasted_iota(jnp.int32, (W, W), 1) + W
    link = first == ids.astype(jnp.float32)
    linked = jnp.sum(jnp.where(link, 1.0, 0.0), axis=0, keepdims=True) > 0.0
    link = as_hot(link)
    second = split(mn[1].reshape(W, W))
    for h in range(ST):
        hi, lo = split(tt[0, h].reshape(WIDE, W))
        raw = jnp.where(linked, dot(hi, link, 1, 0) + dot(lo, link, 1, 0), tt[1, h].reshape(WIDE, W))
        t1[h * WIDE:(h + 1) * WIDE, :] = raw - dot3(solved[h], second)
    for j in range(2):
        for k, block in enumerate(swap(1, j, t1[...])):
            o_buf[j, k] = block
    mixed = split(lax.dot_general(inv_ref[1], mn[0].reshape(W, W), (((1,), (0,)), ((), ())),
                                  precision=lax.Precision.HIGHEST, preferred_element_type=jnp.float32))
    drop = [dot3(solved[h], mixed) for h in range(ST)]
    settle(x_copies[1])
    low = [below(1, j) for j in range(2)]
    for h in range(ST):
        upper[1, h].wait_recv()
        solved1 = ut[1, h].reshape(WIDE, W) - drop[h]
        u1[h * WIDE:(h + 1) * WIDE, :] = solved1
        solved1 = split(solved1)
        for j in range(2):
            product = dot3(low[j], solved1)
            at = h * (W // 2)
            part = pl.ds(at, W // 2)
            o_buf[j, 2 * h] = o_buf[j, 2 * h] - product[:, at:at + W]
            rest = product[:, :W // 2] if h else product[:, W:]
            o_buf[j, 1, :, part] = o_buf[j, 1, :, part] - rest

    @pl.when(p == 1)
    def _():
        for k in range(KB):
            o_buf[0, k] = u1[k * W:(k + 1) * W, :].T

    store = pltpu.make_async_copy(o_buf, o_hbm, out_sem)
    store.start()
    for copy in sent:
        copy.wait_send()
    for s in range(2):
        @pl.when(p == s)
        def _():
            for t in range(2 * NY):
                if t != s:
                    piece = tsrc.at[s, :, t % 2, t // 2]
                    pltpu.make_async_remote_copy(src_ref=piece, dst_ref=piece, send_sem=ts_s.at[s, t],
                                                 recv_sem=ts_r.at[s], device_id=mate, device_id_type=MESH).wait_send()
    for n, h in enumerate(HOLDERS):
        @pl.when(q == h)
        def _():
            @pl.loop(1, NQ)
            def _(i):
                piece = loc.at[pl.ds(0, PR)]
                pltpu.make_async_remote_copy(src_ref=piece, dst_ref=piece, send_sem=sc_s.at[i], recv_sem=sc_r.at[n],
                                             device_id=mate, device_id_type=MESH).wait_send()

    @pl.when(lined)
    def _():
        remote(et.at[1 - c], ep, e_s.at[0], e_r.at[0], mate).wait_send()
        for i in range(1, NY):
            remote(es.at[chip(i)], er.at[i - 1], e_s.at[i], e_r.at[i], at_y(i)).wait_send()

        @pl.when(p == 1)
        def _():
            for t in range(2 * NY):
                if t != 1:
                    remote(loc.at[pl.ds(0, PR)], ms.at[1], n_s.at[t], n_r, mate).wait_send()

    for n in range(2):
        @pl.when(q == HOLDERS[n])
        def _():
            for i in range(1, NX):
                remote(mr.at[n], mr.at[n], m_s.at[i], m_r.at[n], mate).wait_send()

        @pl.when(z == HOLDERS[n] % NZ)
        def _():
            for i in range(1, NZ):
                remote(mr.at[n], mr.at[n], m_s.at[NX + i], m_r.at[n], mate).wait_send()
    store.wait()


def body(matrix, lower_panel, inverses, pivots, panel_owner):
    f32 = jnp.float32
    dma = pltpu.SemaphoreType.DMA
    blocks = matrix.transpose(0, 2, 1, 3)
    any_spec = pl.BlockSpec(memory_space=pl.ANY)
    line = (ST, 2, NY, SL, W)
    out = pl.pallas_call(
        kernel,
        out_shape=jax.ShapeDtypeStruct(blocks.shape, f32),
        in_specs=[any_spec] * 5,
        out_specs=any_spec,
        scratch_shapes=[
            pltpu.VMEM((2, KB, W, W), f32),
            pltpu.VMEM((2 * W, W), f32),
            pltpu.VMEM((2, W, W), f32),
            pltpu.VMEM((2, W), jnp.int32),
            pltpu.SMEM((2,), jnp.int32),
            pltpu.VMEM((2,) + line, f32),
            pltpu.VMEM((2, ST, NY, SL, W), f32),
            pltpu.VMEM((2, ST, NY, SL, W), f32),
            pltpu.VMEM((2, ST, 3, SL, W), f32),
            pltpu.VMEM((2, ST, 2, SL, W), f32),
            pltpu.VMEM((2, ST, 2, SL, W), f32),
            pltpu.VMEM((2, ST, 2, SL, W), f32),
            pltpu.VMEM((2, ST, 2, SL, W), f32),
            pltpu.VMEM((2,) + line, f32),
            pltpu.VMEM((2,) + line, f32),
            pltpu.VMEM((2,) + line, f32),
            pltpu.VMEM((3, PR, W), f32),
            pltpu.VMEM((2, 2 * W, W), f32),
            pltpu.VMEM((2, NY, PR, W), f32),
            pltpu.VMEM((NY, PR, W), f32),
            pltpu.VMEM((NY, PR, W), f32),
            pltpu.VMEM((NY - 1, PR, W), f32),
            pltpu.VMEM((2, PR, W), f32),
            pltpu.VMEM((2, 2, PR, W), f32),
            pltpu.VMEM((2, 2, NY, PR, W), f32),
            pltpu.VMEM((KB * W, W), f32),
            pltpu.VMEM((KB * W, W), f32),
            pltpu.VMEM((2, KB, W, W), f32),
            dma((5,)), dma(()),
            dma((2, ST)), dma((2, ST)),
            dma((2, ST, 7)), dma((2, ST, 7)),
            dma((2, 2 * NY)), dma((2,)),
            dma((7, 7)), dma((7, 7)),
            dma((7,)), dma((7,)),
            dma((NQ,)), dma((3,)),
            dma((2, NZ)), dma((2, NZ)),
            dma((2, NX)), dma((2, NX)),
            dma((NY,)), dma((NY,)),
            dma((2 * NY,)), dma(()),
            dma((NX + NZ,)), dma((2,)),
        ],
        compiler_params=pltpu.CompilerParams(collective_id=0, has_side_effects=True, vmem_limit_bytes=60 * 2**20),
    )(blocks, lower_panel.reshape(2 * W, W), inverses, pivots, panel_owner)
    return out.transpose(0, 2, 1, 3)


def solution(mesh):
    in_specs = (P(None, "prow", None, "pcol"), P(None, "prow", "pcol"), P(), P(), P())
    return jax.shard_map(body, mesh=mesh, in_specs=in_specs, out_specs=P(None, "prow", None, "pcol"), check_vma=False)
```

time: 451 us -> 70 us (0.16)
  waiting for transfers between devices: 397 us -> 0 us
  Pallas kernels: 0 us -> 67.1 us
  local copies, waits for them, and re-layouts: 26.8 us -> 2.74 us
  between operations: 14.8 us -> 0.01 us
  matrix products: 7.36 us -> 0 us
  other arithmetic: 5.39 us -> 0 us
    psum x3 -> x0, waiting for transfers between devices: 397 us -> none  [spread(): return lax.psum(block, axis)]
    pallas_call x0 -> x1, Pallas kernels: none -> 67.1 us  [body(): pl.pallas_call(kernel, out_shape=jax.ShapeDtypeStruct(blocks.shape, f32),...]
    scatter x5 -> x0, local copies, waits for them, and re-layouts: 8.1 us -> none  [the longest x4 7.64 us: body(): current = current.at[landing].set(top_block, mode='drop')]
    dot_general x4 -> x0, matrix products: 7.36 us -> none  [the longest x2 5.73 us: body(): current = current - jnp.dot(masked, upper, precision=lax.Precision.HIGHEST)]
    reshape x3 -> x0, local copies, waits for them, and re-layouts: 6.92 us -> none  [the longest x1 3.83 us: body(): current = matrix.reshape(row_count, col_count)]
    select_n x9 -> x0, other arithmetic: 5.14 us -> none  [the longest x3 3.22 us: spread(): jnp.where(lax.axis_index(axis) == holder, block, jnp.zeros_like(block))]
    gather x4 -> x0, local copies, waits for them, and re-layouts: 4.71 us -> none  [body(): offered = jnp.where(owned[:, None], current[safe_rows], 0.0)]
  transfers between devices with their start and end apart: 3 -> 0, of which waited for: 3 -> 0; matrix products, arithmetic and copies ran while one was open for 2% -> 0% of each run, Pallas kernels for 0% -> 0%
where the time goes in v3:
time: 70 us; the launch traced here: 69.8 us
  Pallas kernels  67.1 us (96%)
  local copies, waits for them, and re-layouts  2.74 us (4%)
    pallas_call x1, Pallas kernels, body(): pl.pallas_call(kernel, out_shape=jax.ShapeDtypeStruct(blocks.shape, f32),...  67.1 us
    unnamed x1, local copies, waits for them, and re-layouts  2.74 us

profile of v3, /device:TPU:1, one launch (start us, length us, event | category | flops | bytes accessed | tf_op | source)
XLA Modules:
  0.0 69.8 jit_solution(11116076782512296832)
XLA Ops:
  0.0 67.1 %shard_map.55 = f32[2,3,256,256]{3,2,1,0:T(8,128)} custom-call(f32[2,3,256,256]{3,2,1,0:T(8,128)} %bitcast.4, f32[512,256]{1,0:T(8,128)} %bitcast.5, f32[2,256,256]{2,1,0:T(8,128)} %inv_hbm.1, s32[2,256]{1,0:T(2,128)} %piv_hbm.1, s32[2]{0:T(128)} %own_hbm.1), custom_call_target="tpu_custom_call" | custom-call | tf_op jit(solution)/shard_map/pallas_call | solution.py:473
  67.1 2.7 %copy.7 = f32[2,256,3,256]{3,1,2,0:T(8,128)} copy(f32[2,256,3,256]{3,1,2,0:T(8,128)} %bitcast.3) | data formatting | bytes 3145728

commit v4 on v3

--- a/solution.py
+++ b/solution.py
@@ -321,6 +321,19 @@
     def rows_piece(step):
         return mn.at[:, c, chip(step)]
 
+    def rows_near(i):
+        return [send(rows_piece(0), rows_piece(0), ag_s.at[i, n], ag_r.at[i, n], at_y(to))
+                for n, to in enumerate((2, -2, 1, -1))]
+
+    def rows_far(i, near):
+        copies = near[2:]
+        for n, to in enumerate((1, -1)):
+            near[n].wait_recv()
+            piece = rows_piece(-2 * to)
+            copies.append(send(piece, piece, ag_s.at[i, 4 + n], ag_r.at[i, 4 + n], at_y(to)))
+        over = rows_piece(-2 * side)
+        return copies + [send(over, over, ag_s.at[i, 6], ag_r.at[i, 6], at_y(2 * side))]
+
     every = [(s, h) for s in range(2) for h in range(ST)]
     slot = {(s, h): 3 * s + h for s, h in every}
 
@@ -334,44 +347,51 @@
     pt[1] = pick(jnp.where(moved, place.astype(jnp.int32), piv_ref[1:2, :]))
     pairs.update({(1, h): pair_up(1, h) for h in range(ST)})
 
+    rows_second()
     work = {k: reduce_first(*k, pairs[k]) for k in every}
-    rows_second()
     for n in range(len(HOLDERS)):
         scatter(n)
     for s in range(2):
         spread_top(s)
+    rows_third()
     work = {k: reduce_second(*k, work[k]) for k in every}
-    rows_third()
+    rows_fourth()
     for n in range(len(HOLDERS)):
         arrived(n)
     z_copies = [gather_z(i) for i in range(2)]
     work = {k: reduce_third(*k, work[k]) for k in every}
-    rows_fourth()
+    tops = [gather_top(s) for s in range(2)]
     upper = {}
     for k in every:
         solve(*k, work[k])
         upper[k] = gather_first(upper_piece(*k), slot[k])
-    tops = [gather_top(s) for s in range(2)]
+    rows_here()
+    rows = rows_near(6)
+    tops = [gather_second(top_piece(s), 3 * s + 2, tops[s]) for s in range(2)]
+    upper = {k: gather_second(upper_piece(*k), slot[k], upper[k]) for k in every}
     x_copies = []
-    for i in range(2):
-        settle(z_copies[i])
-        x_copies.append(gather_x(i))
-    upper = {k: gather_second(upper_piece(*k), slot[k], upper[k]) for k in every}
-    tops = [gather_second(top_piece(s), 3 * s + 2, tops[s]) for s in range(2)]
-    rows_here()
-    rows = gather_first(rows_piece, 6)
+    settle(z_copies[0])
+    x_copies.append(gather_x(0))
+    rows = rows_far(6, rows)
+    tops = [gather_third(top_piece(s), 3 * s + 2, tops[s]) for s in range(2)]
     upper = {k: gather_third(upper_piece(*k), slot[k], upper[k]) for k in every}
-    tops = [gather_third(top_piece(s), 3 * s + 2, tops[s]) for s in range(2)]
-    rows = gather_second(rows_piece, 6, rows)
+    settle(z_copies[1])
+    x_copies.append(gather_x(1))
+    rows = share(mn.at[:, c], 6, rows)
     upper = {k: share(ut.at[k[0], k[1], c], slot[k], upper[k]) for k in every}
-    rows = gather_third(rows_piece, 6, rows)
     tops = [share(tt.at[s, :, c], 3 * s + 2, tops[s]) for s in range(2)]
-    rows = share(mn.at[:, c], 6, rows)
-
-    settle(tops)
-    settle(x_copies[0])
+
     for h in range(ST):
         upper[0, h].wait_recv()
+    solved = [split(ut[0, h].reshape(WIDE, W)) for h in range(ST)]
+    rows.wait_recv()
+    mixed = split(lax.dot_general(inv_ref[1], mn[0].reshape(W, W), (((1,), (0,)), ((), ())),
+                                  precision=lax.Precision.HIGHEST, preferred_element_type=jnp.float32))
+    drop = [dot3(solved[h], mixed) for h in range(ST)]
+    second = split(mn[1].reshape(W, W))
+    drop_top = [dot3(solved[h], second) for h in range(ST)]
+    settle(x_copies[0])
+    tops[0].wait_recv()
     for j in range(2):
         update(j)
 
@@ -381,23 +401,18 @@
         for k in range(KB):
             a[0, k] = whole[k * W:(k + 1) * W].T
 
-    rows.wait_recv()
-    solved = [split(ut[0, h].reshape(WIDE, W)) for h in range(ST)]
     ids = lax.broadcasted_iota(jnp.int32, (W, W), 1) + W
     link = first == ids.astype(jnp.float32)
     linked = jnp.sum(jnp.where(link, 1.0, 0.0), axis=0, keepdims=True) > 0.0
     link = as_hot(link)
-    second = split(mn[1].reshape(W, W))
+    tops[1].wait_recv()
     for h in range(ST):
         hi, lo = split(tt[0, h].reshape(WIDE, W))
         raw = jnp.where(linked, dot(hi, link, 1, 0) + dot(lo, link, 1, 0), tt[1, h].reshape(WIDE, W))
-        t1[h * WIDE:(h + 1) * WIDE, :] = raw - dot3(solved[h], second)
+        t1[h * WIDE:(h + 1) * WIDE, :] = raw - drop_top[h]
     for j in range(2):
         for k, block in enumerate(swap(1, j, t1[...])):
             o_buf[j, k] = block
-    mixed = split(lax.dot_general(inv_ref[1], mn[0].reshape(W, W), (((1,), (0,)), ((), ())),
-                                  precision=lax.Precision.HIGHEST, preferred_element_type=jnp.float32))
-    drop = [dot3(solved[h], mixed) for h in range(ST)]
     settle(x_copies[1])
     low = [below(1, j) for j in range(2)]
     for h in range(ST):

time: 70 us -> 66.6 us (0.951)
  Pallas kernels: 67.1 us -> 63.7 us
    pallas_call x1, Pallas kernels: 67.1 us -> 63.7 us  [body(): pl.pallas_call(kernel, out_shape=jax.ShapeDtypeStruct(blocks.shape, f32),...]
where the time goes in v4:
time: 66.6 us; the launch traced here: 66.4 us
  Pallas kernels  63.7 us (96%)
  local copies, waits for them, and re-layouts  2.74 us (4%)
    pallas_call x1, Pallas kernels, body(): pl.pallas_call(kernel, out_shape=jax.ShapeDtypeStruct(blocks.shape, f32),...  63.7 us
    unnamed x1, local copies, waits for them, and re-layouts  2.74 us

profile of v4, /device:TPU:1, one launch (start us, length us, event | category | flops | bytes accessed | tf_op | source)
XLA Modules:
  0.0 66.4 jit_solution(6824858336108373029)
XLA Ops:
  0.0 63.7 %shard_map.55 = f32[2,3,256,256]{3,2,1,0:T(8,128)} custom-call(f32[2,3,256,256]{3,2,1,0:T(8,128)} %bitcast.4, f32[512,256]{1,0:T(8,128)} %bitcast.5, f32[2,256,256]{2,1,0:T(8,128)} %inv_hbm.1, s32[2,256]{1,0:T(2,128)} %piv_hbm.1, s32[2]{0:T(128)} %own_hbm.1), custom_call_target="tpu_custom_call" | custom-call | tf_op jit(solution)/shard_map/pallas_call | solution.py:488
  63.7 2.7 %copy.7 = f32[2,256,3,256]{3,1,2,0:T(8,128)} copy(f32[2,256,3,256]{3,1,2,0:T(8,128)} %bitcast.3) | data formatting | bytes 3145728

commit v5 on v4

--- a/solution.py
+++ b/solution.py
@@ -206,6 +206,18 @@
             copies.append(send(piece(-2 * to), piece(-2 * to), ag_s.at[i, 4 + n], ag_r.at[i, 4 + n], at_y(to)))
         over = piece(-2 * side)
         return copies + [send(over, over, ag_s.at[i, 6], ag_r.at[i, 6], at_y(2 * side))]
+
+    def ring_third(piece, i, second):
+        copies = []
+        for n, to in enumerate((1, -1)):
+            second[n].wait_recv()
+            copies.append(send(piece(-2 * to), piece(-2 * to), ag_s.at[i, 4 + n], ag_r.at[i, 4 + n], at_y(to)))
+        return copies
+
+    def ring_fourth(piece, i, third):
+        settle(third)
+        last = piece(-3 * side)
+        return [send(last, last, ag_s.at[i, 6], ag_r.at[i, 6], at_y(side))]
 
     def share(half, i, far):
         settle(far)
@@ -373,8 +385,9 @@
     settle(z_copies[0])
     x_copies.append(gather_x(0))
     rows = rows_far(6, rows)
-    tops = [gather_third(top_piece(s), 3 * s + 2, tops[s]) for s in range(2)]
+    tops = [ring_third(top_piece(s), 3 * s + 2, tops[s]) for s in range(2)]
     upper = {k: gather_third(upper_piece(*k), slot[k], upper[k]) for k in every}
+    tops = [ring_fourth(top_piece(s), 3 * s + 2, tops[s]) for s in range(2)]
     settle(z_copies[1])
     x_copies.append(gather_x(1))
     rows = share(mn.at[:, c], 6, rows)

time: 66.6 us -> 66.1 us (level)
  no operation moved by 1% of the time
where the time goes in v5:
time: 66.1 us; the launch traced here: 65.9 us
  Pallas kernels  63.2 us (96%)
  local copies, waits for them, and re-layouts  2.74 us (4%)
    pallas_call x1, Pallas kernels, body(): pl.pallas_call(kernel, out_shape=jax.ShapeDtypeStruct(blocks.shape, f32),...  63.2 us
    unnamed x1, local copies, waits for them, and re-layouts  2.74 us

profile of v5, /device:TPU:1, one launch (start us, length us, event | category | flops | bytes accessed | tf_op | source)
XLA Modules:
  0.0 65.9 jit_solution(5921262828710842888)
XLA Ops:
  0.0 63.2 %shard_map.55 = f32[2,3,256,256]{3,2,1,0:T(8,128)} custom-call(f32[2,3,256,256]{3,2,1,0:T(8,128)} %bitcast.4, f32[512,256]{1,0:T(8,128)} %bitcast.5, f32[2,256,256]{2,1,0:T(8,128)} %inv_hbm.1, s32[2,256]{1,0:T(2,128)} %piv_hbm.1, s32[2]{0:T(128)} %own_hbm.1), custom_call_target="tpu_custom_call" | custom-call | tf_op jit(solution)/shard_map/pallas_call | solution.py:501
  63.2 2.7 %copy.7 = f32[2,256,3,256]{3,1,2,0:T(8,128)} copy(f32[2,256,3,256]{3,1,2,0:T(8,128)} %bitcast.3) | data formatting | bytes 3145728

commit v6 on v5

--- a/solution.py
+++ b/solution.py
@@ -74,11 +74,11 @@
         for copy in copies:
             copy.wait_recv()
 
-    load_a = pltpu.make_async_copy(a_hbm, a, load_sem.at[0])
-    load_p = pltpu.make_async_copy(piv_hbm, piv_ref, load_sem.at[1])
-    load_rest = [pltpu.make_async_copy(src, dst, load_sem.at[2 + i]) for i, (src, dst) in enumerate(
+    load_a = [pltpu.make_async_copy(a_hbm.at[:, k], a.at[:, k], load_sem.at[4 + k]) for k in range(KB)]
+    load_p = pltpu.make_async_copy(piv_hbm, piv_ref, load_sem.at[0])
+    load_rest = [pltpu.make_async_copy(src, dst, load_sem.at[1 + i]) for i, (src, dst) in enumerate(
         ((l_hbm, loc), (inv_hbm, inv_ref), (own_hbm, own_ref)))]
-    for copy in [load_p, load_a] + load_rest:
+    for copy in [load_p] + load_a + load_rest:
         copy.start()
 
     barrier = pltpu.get_barrier_semaphore()
@@ -98,10 +98,12 @@
         rows = lax.broadcasted_iota(jnp.int32, (W, W), 0) + (j * 2 * NY + p) * W
         return rows == wanted
 
-    def pick(wanted):
+    def pick(wanted, loads=()):
         hot = [as_hot(onehot(j, wanted)) for j in range(2)]
         blocks = []
         for k in range(KB):
+            for copy in loads[k:k + 1]:
+                copy.wait()
             total = jnp.zeros((W, W), jnp.float32)
             for j in range(2):
                 for part in split(a[j, k]):
@@ -110,8 +112,7 @@
         return jnp.concatenate(blocks, axis=0).reshape(ST, 2, NY, SL, W)
 
     load_p.wait()
-    load_a.wait()
-    pt[0] = pick(piv_ref[0:1, :])
+    pt[0] = pick(piv_ref[0:1, :], load_a)
 
     holds = jnp.logical_or(q == HOLDERS[0], jnp.logical_or(q == HOLDERS[1], q == HOLDERS[2]))
     heard = len(greet) + jnp.where(holds, NQ - 1, 0) + jnp.where(y == 0, NY - 1, 0)
@@ -428,6 +429,15 @@
             o_buf[j, k] = block
     settle(x_copies[1])
     low = [below(1, j) for j in range(2)]
+    stores = []
+
+    def finish(k):
+        @pl.when(p == 1)
+        def _():
+            o_buf[0, k] = u1[k * W:(k + 1) * W, :].T
+        stores.append(pltpu.make_async_copy(o_buf.at[:, k], o_hbm.at[:, k], out_sem.at[k]))
+        stores[-1].start()
+
     for h in range(ST):
         upper[1, h].wait_recv()
         solved1 = ut[1, h].reshape(WIDE, W) - drop[h]
@@ -440,14 +450,11 @@
             o_buf[j, 2 * h] = o_buf[j, 2 * h] - product[:, at:at + W]
             rest = product[:, :W // 2] if h else product[:, W:]
             o_buf[j, 1, :, part] = o_buf[j, 1, :, part] - rest
-
-    @pl.when(p == 1)
-    def _():
-        for k in range(KB):
-            o_buf[0, k] = u1[k * W:(k + 1) * W, :].T
-
-    store = pltpu.make_async_copy(o_buf, o_hbm, out_sem)
-    store.start()
+        if h == 0:
+            finish(0)
+
+    finish(1)
+    finish(2)
     for copy in sent:
         copy.wait_send()
     for s in range(2):
@@ -489,7 +496,8 @@
         def _():
             for i in range(1, NZ):
                 remote(mr.at[n], mr.at[n], m_s.at[NX + i], m_r.at[n], mate).wait_send()
-    store.wait()
+    for copy in stores:
+        copy.wait()
 
 
 def body(matrix, lower_panel, inverses, pivots, panel_owner):
@@ -532,7 +540,7 @@
             pltpu.VMEM((KB * W, W), f32),
             pltpu.VMEM((KB * W, W), f32),
             pltpu.VMEM((2, KB, W, W), f32),
-            dma((5,)), dma(()),
+            dma((4 + KB,)), dma((KB,)),
             dma((2, ST)), dma((2, ST)),
             dma((2, ST, 7)), dma((2, ST, 7)),
             dma((2, 2 * NY)), dma((2,)),

time: 66.1 us -> 65.9 us (level)
  no operation moved by 1% of the time
where the time goes in v6:
time: 65.9 us; the launch traced here: 65.8 us
  Pallas kernels  63 us (96%)
  local copies, waits for them, and re-layouts  2.74 us (4%)
    pallas_call x1, Pallas kernels, body(): pl.pallas_call(kernel, out_shape=jax.ShapeDtypeStruct(blocks.shape, f32),...  63 us
    unnamed x1, local copies, waits for them, and re-layouts  2.74 us

profile of v6, /device:TPU:1, one launch (start us, length us, event | category | flops | bytes accessed | tf_op | source)
XLA Modules:
  0.0 65.8 jit_solution(8359170340891599389)
XLA Ops:
  0.0 63.0 %shard_map.55 = f32[2,3,256,256]{3,2,1,0:T(8,128)} custom-call(f32[2,3,256,256]{3,2,1,0:T(8,128)} %bitcast.4, f32[512,256]{1,0:T(8,128)} %bitcast.5, f32[2,256,256]{2,1,0:T(8,128)} %inv_hbm.1, s32[2,256]{1,0:T(2,128)} %piv_hbm.1, s32[2]{0:T(128)} %own_hbm.1), custom_call_target="tpu_custom_call" | custom-call | tf_op jit(solution)/shard_map/pallas_call | solution.py:509
  63.0 2.7 %copy.7 = f32[2,256,3,256]{3,1,2,0:T(8,128)} copy(f32[2,256,3,256]{3,1,2,0:T(8,128)} %bitcast.3) | data formatting | bytes 3145728
